TPU v7x, 32 devices: a whole 2x2x4 slice. The times are simulated.
32 devices in a mesh: ctx: 16 (over z, x, core), head: 2 (over y).
Axes of the slice: x: 2, y: 2, z: 4, core: 2. Of those that a mesh axis runs over, the one named last changes fastest.
Arguments:
- query: bfloat16 [4096, 32, 128], P('ctx', 'head'), may hold values from -160 to 160
- key: bfloat16 [4096, 8, 128], P('ctx', 'head'), may hold values from -8 to 8
- value: bfloat16 [4096, 8, 128], P('ctx', 'head'), may hold values from -6 to 6
- d_mixed: bfloat16 [4096, 4096], P('ctx', 'head'), may hold values from -6 to 6
- out_weight: bfloat16 [4096, 4096], P('head'), may hold values from -1 to 1
- block_keys: int32 [32, 20], P('ctx'), may hold values from 0 to 31, as said below
- scope_ids: int32 [4096], P('ctx'), may hold values from 0 to 15
Outputs:
- grad_query: bfloat16 [4096, 32, 128], P('ctx', 'head')
- grad_key: bfloat16 [4096, 8, 128], P('ctx', 'head')
- grad_value: bfloat16 [4096, 8, 128], P('ctx', 'head')
Inputs may be any that keep to these rules, and one draw needn't show every extreme that they name: `block_keys`: row b names 20 distinct key blocks, block b itself among them.
All inputs are finite; a program needn't handle non-finite values.
Results may differ from a plain program's by a relative error of at most 0.0059.
Values may be sent and summed in bfloat16 or wider, within the bound.
A program may use at most 192 MiB of HBM per device.

v0:
```python
import math
import jax
import jax.numpy as jnp
from jax import lax
from jax.sharding import PartitionSpec as P

BLK = 128


def score_pair(q_block, scope_q, k_block, scope_k, scale):
    scores = (
        jnp.einsum("ignd,jgd->gnij", q_block, k_block, preferred_element_type=jnp.float32) * scale
    )
    scope_key = scope_k.astype(jnp.float32)
    visible = (scope_key[None, :] == scope_q[:, None]) | (scope_key[None, :] == 0.0)
    return (scores, visible)


def backward_pair(
    q_block, do_block, lse_here, delta_here, scope_q, k_block, v_block, scope_k, scale
):
    scores, visible = score_pair(q_block, scope_q, k_block, scope_k, scale)
    probs = jnp.where(visible, jnp.exp(scores - lse_here[..., None]), 0.0)
    rounded = probs.astype(jnp.bfloat16)
    grad_v = jnp.einsum("gnij,ignd->jgd", rounded, do_block, preferred_element_type=jnp.float32)
    dprobs = jnp.einsum("ignd,jgd->gnij", do_block, v_block, preferred_element_type=jnp.float32)
    dscores = (probs * (dprobs - delta_here[..., None]) * scale).astype(jnp.bfloat16)
    grad_q = jnp.einsum("gnij,jgd->ignd", dscores, k_block, preferred_element_type=jnp.float32)
    grad_k = jnp.einsum("gnij,ignd->jgd", dscores, q_block, preferred_element_type=jnp.float32)
    return (grad_q, grad_k, grad_v)


def on_device(query, key, value, d_mixed, out_weight, block_keys, scope_ids):
    tokens_here = query.shape[0]
    heads_here = query.shape[1]
    width = query.shape[2]
    kv_here = key.shape[1]
    group = heads_here // kv_here
    blocks = tokens_here // BLK
    scale = 1.0 / math.sqrt(width)
    d_out = lax.dot_general(
        lax.all_gather(d_mixed, "head", axis=1, tiled=True),
        out_weight,
        (((1,), (1,)), ((), ())),
        preferred_element_type=jnp.float32,
    ).astype(jnp.bfloat16)
    q_blocks = query.reshape(blocks, BLK, kv_here, group, width)
    do_blocks = d_out.reshape(blocks, BLK, kv_here, group, width)
    own_scope = scope_ids.reshape(blocks, BLK).astype(jnp.float32)
    all_keys, all_values, all_scope = (
        lax.all_gather(key, "ctx", axis=0, tiled=True),
        lax.all_gather(value, "ctx", axis=0, tiled=True),
        lax.all_gather(scope_ids.astype(jnp.bfloat16), "ctx", axis=0, tiled=True),
    )
    total_blocks = all_keys.shape[0] // BLK
    k_all = all_keys.reshape(total_blocks, BLK, kv_here, width)
    v_all = all_values.reshape(total_blocks, BLK, kv_here, width)
    s_all = all_scope.reshape(total_blocks, BLK)
    slots = block_keys.shape[1]
    grad_k_all = jnp.zeros((total_blocks, BLK, kv_here, width), jnp.float32)
    grad_v_all = jnp.zeros((total_blocks, BLK, kv_here, width), jnp.float32)
    grad_rows = []
    for row in range(blocks):
        listed = block_keys[row]
        k_near = k_all[listed].reshape(slots * BLK, kv_here, width)
        v_near = v_all[listed].reshape(slots * BLK, kv_here, width)
        s_near = s_all[listed].reshape(slots * BLK)
        scores, visible = score_pair(q_blocks[row], own_scope[row], k_near, s_near, scale)
        masked = jnp.where(visible, scores, -1e30)
        high = jnp.max(masked, axis=-1)
        total = jnp.sum(jnp.where(visible, jnp.exp(scores - high[..., None]), 0.0), axis=-1)
        lse_here = high + jnp.log(total)
        probs = jnp.where(visible, jnp.exp(scores - lse_here[..., None]), 0.0)
        attn_out = jnp.einsum(
            "gnij,jgd->ignd", probs, v_near.astype(jnp.float32), precision=lax.Precision.HIGHEST
        )
        delta = jnp.sum(do_blocks[row].astype(jnp.float32) * attn_out, axis=-1)
        delta_here = jnp.transpose(delta, (1, 2, 0))
        grad_q, part_k, part_v = backward_pair(
            q_blocks[row],
            do_blocks[row],
            lse_here,
            delta_here,
            own_scope[row],
            k_near,
            v_near,
            s_near,
            scale,
        )
        grad_rows.append(grad_q)
        grad_k_all = grad_k_all.at[listed].add(part_k.reshape(slots, BLK, kv_here, width))
        grad_v_all = grad_v_all.at[listed].add(part_v.reshape(slots, BLK, kv_here, width))
    combined = jnp.concatenate([grad_k_all, grad_v_all], axis=-1).reshape(
        total_blocks * BLK, kv_here, 2 * width
    )
    home = lax.psum_scatter(combined, "ctx", scatter_dimension=0, tiled=True)
    grad_query = jnp.stack(grad_rows).reshape(tokens_here, heads_here, width).astype(jnp.bfloat16)
    grad_key = home[:, :, :width].astype(jnp.bfloat16)
    grad_value = home[:, :, width:].astype(jnp.bfloat16)
    return (grad_query, grad_key, grad_value)


def solution(mesh):
    in_specs = (
        P("ctx", "head", None),
        P("ctx", "head", None),
        P("ctx", "head", None),
        P("ctx", "head"),
        P("head", None),
        P("ctx", None),
        P("ctx"),
    )
    out_specs = (P("ctx", "head", None), P("ctx", "head", None), P("ctx", "head", None))
    return jax.shard_map(
        on_device, mesh=mesh, in_specs=in_specs, out_specs=out_specs, check_vma=False
    )
```

profile of v0, /device:TPU:0, one launch (start us, length us, event | category | flops | bytes accessed | tf_op | source)
XLA Modules:
  0.0 586.1 jit_solution(16674847419327355169)
XLA Ops:
  7.9 1.7 copy.164
  11.2 23.1 %all-gather = bf16[16,1,256]{2,1,0:T(2,128)(2,1)S(1)} all-gather(bf16[1,1,256]{2,1,0:T(2,128)(2,1)S(1)} %reshape.254), channel_id=1, replica_groups=mesh['ctx'=16,'head'=2] {'ctx'}, dimensions={0}, use_global_device_ids=true | all-gather | bytes 8704 | tf_op jit(solution)/shard_map/all_gather | solution.py:53
  40.2 1.8 compare_or_fusion.1
  41.9 1.8 compare_or_fusion
  43.7 1.7 all-gather.9.cloned.1.call-done
  45.4 10.9 %convolution_convert_fusion = bf16[256,2048]{1,0:T(8,128)(2,1)S(1)} fusion(bf16[256,4096]{1,0:T(8,128)(2,1)} %all-gather.9.cloned.1.call-done, bf16[2048,4096]{1,0:T(8,128)(2,1)} %param.11), kind=kOutput, calls=%fused_computation.55 | convolution fusion | flops 4295491584 | bytes 19922944 | tf_op jit(solution)/shard_map/dot_general | solution.py:41
  58.5 40.3 %all-gather.7.cloned.1.call-done = bf16[4096,4,128]{2,0,1:T(8,128)(2,1)} async-done(((bf16[256,4,128]{2,0,1:T(8,128)(2,1)}), bf16[4096,4,128]{2,0,1:T(8,128)(2,1)}) %all-gather.7.cloned.1.call-update) | async-done | bytes 4194320 | tf_op jit(solution)/shard_map/all_gather | solution.py:52
  98.8 4.7 copy.165
  103.5 3.2 gather_fusion.5
  106.7 4.9 gather_fusion.2
  111.6 38.4 %all-gather.5.cloned.1.call-done = bf16[4096,4,128]{2,1,0:T(4,128)(2,1)} async-done(((bf16[256,4,128]{2,1,0:T(4,128)(2,1)}), bf16[4096,4,128]{2,1,0:T(4,128)(2,1)}) %all-gather.5.cloned.1.call-update) | async-done | bytes 4194320 | tf_op jit(solution)/shard_map/all_gather | solution.py:51
  150.0 7.4 %gather_fusion = bf16[20,128,4,128]{3,2,1,0:T(4,128)(2,1)} fusion(bf16[32,128,4,128]{3,2,1,0:T(4,128)(2,1)} %bitcast.211, s32[1024]{0:T(1024)S(1)} %get-tuple-element.35), kind=kCustom, calls=%fused_computation | custom fusion | bytes 5242960 | tf_op jit(solution)/shard_map/gather | solution.py:65
  157.4 7.6 %gather_fusion.3 = bf16[20,128,4,128]{3,2,1,0:T(4,128)(2,1)} fusion(bf16[32,128,4,128]{3,2,1,0:T(4,128)(2,1)} %bitcast.212, s32[1024]{0:T(1024)S(1)} %get-tuple-element.34), kind=kCustom, calls=%fused_computation.3 | custom fusion | bytes 5242960 | tf_op jit(solution)/shard_map/gather | solution.py:65
  165.1 3.7 copy.166
  168.8 1.7 copy.175
  171.2 2.2 copy.162
  173.4 4.5 fusion.12
  177.9 4.3 fusion.15
  182.2 2.8 copy-done
  185.0 11.8 %fusion.38 = f32[2560,4,128]{0,2,1:T(8,128)} fusion(bf16[128,4,4,128]{0,3,2,1:T(8,128)(2,1)S(1)} %bitcast.226, f32[4,2560,128,4]{2,1,3,0:T(8,128)} %copy-done, f32[4,4,128]{2,1,0:T(4,128)S(1)} %bitcast.233, pred[128,2560]{0,1:T(8,128)(4,1)S(1)} %compare_or_fusion.1), kind=kOutput, calls=%fused_computation.53 | convolution fusion | flops 1363148800 | bytes 27074560 | tf_op jit(solution)/shard_map/gnij,ignd->jgd/dot_general | solution.py:25
  196.8 16.6 %fusion.61 = f32[128,4,4]{0,2,1:T(4,128)S(1)} fusion(bf16[2560,4,128,1]{2,0,3,1:T(8,128)(2,1)S(1)} %bitcast.221, f32[4,2560,128,4]{2,1,3,0:T(8,128)} %copy-done, f32[4,4,128]{2,1,0:T(4,128)S(1)} %bitcast.234, pred[128,2560]{0,1:T(8,128)(4,1)S(1)} %compare_or_fusion.1, bf16[128,4,4,128]{0,3,2,1:T(8,128)(2,1)S(1)} %bitcast.227), kind=kOutput, calls=%fused_computation.67 | convolution fusion | flops 8069576704 | bytes 24461312 | tf_op jit(solution)/shard_map/gnij,jgd->ignd/dot_general | solution.py:74
  213.4 15.1 %fusion.11 = bf16[4,4,128,2560]{2,3,1,0:T(8,128)(2,1)} fusion(f32[4,2560,128,4]{2,1,3,0:T(8,128)} %copy-done, f32[4,4,128]{2,1,0:T(4,128)S(1)} %bitcast.239, f32[4,4,128]{2,1,0:T(4,128)S(1)} %bitcast.235, pred[128,2560]{0,1:T(8,128)(4,1)S(1)} %compare_or_fusion.1, bf16[2560,4,128,1]{2,0,3,1:T(8,128)(2,1)S(1)} %bitcast.222, ...), kind=kOutput, calls=%fused_computation.26 | convolution fusion | flops 1378877440 | bytes 34947072 | tf_op jit(solution)/shard_map/ignd,jgd->gnij/dot_general | solution.py:26
  228.5 5.6 fusion.79
  234.1 2.9 copy.182
  237.0 6.3 %copy.186 = f32[2560,4,128]{2,0,1:T(8,128)} copy(f32[2560,4,128]{0,2,1:T(8,128)} %fusion.38) | data formatting | bytes 10485760 | tf_op jit(solution)/shard_map/gnij,ignd->jgd/transpose | solution.py:25
  243.4 5.5 copy.187
  248.8 3.0 fusion.3
  251.8 4.3 fusion.6
  256.2 2.8 copy-done.1
  259.0 11.9 %fusion.41 = f32[2560,4,128]{0,2,1:T(8,128)} fusion(bf16[128,4,4,128]{0,3,2,1:T(8,128)(2,1)S(1)} %bitcast.223, f32[4,2560,128,4]{2,1,3,0:T(8,128)} %copy-done.1, f32[4,4,128]{2,1,0:T(4,128)S(1)} %bitcast.236, pred[128,2560]{0,1:T(8,128)(4,1)S(1)} %compare_or_fusion), kind=kOutput, calls=%fused_computation.54 | convolution fusion | flops 1363148800 | bytes 27074560 | tf_op jit(solution)/shard_map/gnij,ignd->jgd/dot_general | solution.py:25
  270.8 16.8 %fusion.58 = f32[128,4,4]{0,2,1:T(4,128)S(1)} fusion(bf16[2560,4,128,1]{2,0,3,1:T(8,128)(2,1)S(1)} %bitcast.219, f32[4,2560,128,4]{2,1,3,0:T(8,128)} %copy-done.1, f32[4,4,128]{2,1,0:T(4,128)S(1)} %bitcast.237, pred[128,2560]{0,1:T(8,128)(4,1)S(1)} %compare_or_fusion, bf16[128,4,4,128]{0,3,2,1:T(8,128)(2,1)S(1)} %bitcast.224), kind=kOutput, calls=%fused_computation.66 | convolution fusion | flops 8069576704 | bytes 24461312 | tf_op jit(solution)/shard_map/gnij,jgd->ignd/dot_general | solution.py:74
  287.6 15.1 %fusion.2 = bf16[4,4,128,2560]{2,3,1,0:T(8,128)(2,1)} fusion(f32[4,2560,128,4]{2,1,3,0:T(8,128)} %copy-done.1, f32[4,4,128]{2,1,0:T(4,128)S(1)} %bitcast.240, f32[4,4,128]{2,1,0:T(4,128)S(1)} %bitcast.238, pred[128,2560]{0,1:T(8,128)(4,1)S(1)} %compare_or_fusion, bf16[2560,4,128,1]{2,0,3,1:T(8,128)(2,1)S(1)} %bitcast.220, ...), kind=kOutput, calls=%fused_computation.13 | convolution fusion | flops 1378877440 | bytes 34947072 | tf_op jit(solution)/shard_map/ignd,jgd->gnij/dot_general | solution.py:26
  302.7 5.6 fusion.80
  308.3 2.9 copy.183
  311.2 5.9 %copy.190 = f32[2560,4,128]{2,0,1:T(8,128)} copy(f32[2560,4,128]{0,2,1:T(8,128)} %fusion.41) | data formatting | bytes 10485760 | tf_op jit(solution)/shard_map/gnij,ignd->jgd/transpose | solution.py:25
  317.1 5.5 copy.191
  322.6 4.3 broadcast.69.clone.1
  326.9 13.7 %scatter_fusion = f32[32,128,4,128]{3,1,2,0:T(8,128)} fusion(f32[32,128,4,128]{3,1,2,0:T(8,128)} %broadcast.69.clone.1, s32[20]{0:T(128)S(1)} %copy-done.13, f32[20,128,4,128]{3,1,2,0:T(8,128)} %copy.182), kind=kCustom, calls=%fused_computation.6 | custom fusion | flops 1310720 | bytes 15728720 | tf_op jit(solution)/shard_map/scatter-add | solution.py:91
  340.7 4.4 broadcast.69.clone
  345.0 13.5 %scatter_fusion.2 = f32[32,128,4,128]{3,1,2,0:T(8,128)} fusion(f32[32,128,4,128]{3,1,2,0:T(8,128)} %broadcast.69.clone, s32[20]{0:T(128)S(1)} %copy-done.13, f32[20,128,4,128]{3,1,2,0:T(8,128)} %copy.187), kind=kCustom, calls=%fused_computation.8 | custom fusion | flops 1310720 | bytes 15728720 | tf_op jit(solution)/shard_map/scatter-add | solution.py:92
  358.6 13.7 %scatter_fusion.1 = f32[32,128,4,128]{3,1,2,0:T(8,128)} fusion(f32[32,128,4,128]{3,1,2,0:T(8,128)} %scatter_fusion, s32[20]{0:T(128)S(1)} %copy-done.11, f32[20,128,4,128]{3,1,2,0:T(8,128)} %copy.183), kind=kCustom, calls=%fused_computation.7 | custom fusion | flops 1310720 | bytes 15728720 | tf_op jit(solution)/shard_map/scatter-add | solution.py:91
  372.2 13.6 %scatter_fusion.3 = f32[32,128,4,128]{3,1,2,0:T(8,128)} fusion(f32[32,128,4,128]{3,1,2,0:T(8,128)} %scatter_fusion.2, s32[20]{0:T(128)S(1)} %copy-done.11, f32[20,128,4,128]{3,1,2,0:T(8,128)} %copy.191), kind=kCustom, calls=%fused_computation.9 | custom fusion | flops 1310720 | bytes 15728720 | tf_op jit(solution)/shard_map/scatter-add | solution.py:92
  385.9 6.6 %pad_maximum_fusion = f32[32,128,4,256]{3,1,2,0:T(8,128)S(1)} fusion(f32[32,128,4,128]{3,1,2,0:T(8,128)} %scatter_fusion.3, f32[32,128,4,128]{3,1,2,0:T(8,128)} %scatter_fusion.1), kind=kLoop, calls=%fused_computation.36 | loop fusion | flops 4194304 | bytes 33554432 | tf_op jit(solution)/shard_map/concatenate | solution.py:93
  392.5 6.1 %copy.192 = f32[32,128,4,256]{3,1,0,2:T(8,128)} copy(f32[32,128,4,256]{3,1,2,0:T(8,128)S(1)} %pad_maximum_fusion) | data formatting | bytes 33554432 | tf_op jit(solution)/shard_map/concatenate | solution.py:93
  398.6 8.9 %fusion.56 = bf16[1,128,4,4,128]{4,1,3,2,0:T(8,128)(2,1)S(1)} fusion(bf16[2560,4,128,1]{2,0,3,1:T(8,128)(2,1)} %bitcast.206, bf16[4,4,128,2560]{2,3,1,0:T(8,128)(2,1)} %fusion.11), kind=kOutput, calls=%fused_computation.64 | convolution fusion | flops 1342439424 | bytes 13631488 | tf_op jit(solution)/shard_map/gnij,jgd->ignd/dot_general | solution.py:28
  407.6 9.4 %fusion.57 = bf16[1,128,4,4,128]{4,1,3,2,0:T(8,128)(2,1)S(1)} fusion(bf16[2560,4,128,1]{2,0,3,1:T(8,128)(2,1)S(1)} %bitcast.204, bf16[4,4,128,2560]{2,3,1,0:T(8,128)(2,1)} %fusion.2), kind=kOutput, calls=%fused_computation.65 | convolution fusion | flops 1342439424 | bytes 13631488 | tf_op jit(solution)/shard_map/gnij,jgd->ignd/dot_general | solution.py:28
  417.2 1.7 copy.193
  418.9 157.1 %reduce-scatter.2.cloned.1.call-done = f32[256,4,256]{2,0,1:T(8,128)} async-done(((f32[4096,4,256]{2,0,1:T(8,128)}), f32[256,4,256]{2,0,1:T(8,128)}) %reduce-scatter.2.cloned.1.call-update) | async-done | bytes 1048592 | tf_op jit(solution)/shard_map/reduce_scatter | solution.py:96
  (62 shorter events, 14.4 us)
Async XLA Ops:
  7.2 38.2 %all-gather.9.cloned.1.call-start = ((), (), s32[]{:S(2)}) async-start(), calls=%async_computation.3 | async-start | bytes 3145728 | tf_op jit(solution)/shard_map/all_gather | solution.py:42
  7.9 90.9 %all-gather.7.cloned.1.call-start = ((), (), s32[]{:S(2)}) async-start(), calls=%async_computation.2 | async-start | bytes 4456448 | tf_op jit(solution)/shard_map/all_gather | solution.py:52
  9.7 140.4 %all-gather.5.cloned.1.call-start = ((), (), s32[]{:S(2)}) async-start(), calls=%async_computation.1 | async-start | bytes 4456448 | tf_op jit(solution)/shard_map/all_gather | solution.py:51
  10.4 565.6 %reduce-scatter.2.cloned.1.call-start = ((), (), s32[]{:S(2)}) async-start(), calls=%async_computation.4 | async-start | bytes 17825792 | tf_op jit(solution)/shard_map/reduce_scatter | solution.py:96
  35.1 0.6 copy-start.10
  35.1 0.6 copy-start.12
  165.1 5.4 copy-start.3
  165.1 6.1 %copy-start.2 = (bf16[20,128,4,128]{3,2,1,0:T(4,128)(2,1)S(1)}, bf16[20,128,4,128]{3,2,1,0:T(4,128)(2,1)}, u32[]{:S(2)}) copy-start(bf16[20,128,4,128]{3,2,1,0:T(4,128)(2,1)} %gather_fusion) | copy-start | bytes 7864324
  165.1 8.3 %copy-start.5 = (bf16[128,16,128]{2,0,1:T(8,128)(2,1)S(1)}, bf16[128,16,128]{2,0,1:T(8,128)(2,1)}, u32[]{:S(2)}) copy-start(bf16[128,16,128]{2,0,1:T(8,128)(2,1)} %copy.163) | copy-start | bytes 1572868
  177.9 7.1 %copy-start = (f32[4,2560,128,4]{2,1,3,0:T(8,128)}, f32[4,2560,128,4]{2,1,3,0:T(8,128)S(1)}, u32[]{:S(2)}) copy-start(f32[4,2560,128,4]{2,1,3,0:T(8,128)S(1)} %get-tuple-element.33) | copy-start | bytes 62914564
  177.9 7.1 %copy-start.9 = (bf16[128,2048]{0,1:T(8,128)(2,1)S(1)}, bf16[128,2048]{0,1:T(8,128)(2,1)}, u32[]{:S(2)}) copy-start(bf16[128,2048]{0,1:T(8,128)(2,1)} %copy.216) | copy-start | bytes 1572868
  185.0 11.8 %copy-start.7 = (bf16[20,128,4,128]{3,1,0,2:T(8,128)(2,1)S(1)}, bf16[20,128,4,128]{3,1,0,2:T(8,128)(2,1)}, u32[]{:S(2)}) copy-start(bf16[20,128,4,128]{3,1,0,2:T(8,128)(2,1)} %copy.166) | copy-start | bytes 7864324
  237.0 11.8 %copy-start.4 = (bf16[128,16,128]{2,0,1:T(8,128)(2,1)S(1)}, bf16[128,16,128]{2,0,1:T(8,128)(2,1)}, u32[]{:S(2)}) copy-start(bf16[128,16,128]{2,0,1:T(8,128)(2,1)} %copy.173) | copy-start | bytes 1572868
  251.8 7.1 %copy-start.1 = (f32[4,2560,128,4]{2,1,3,0:T(8,128)}, f32[4,2560,128,4]{2,1,3,0:T(8,128)S(1)}, u32[]{:S(2)}) copy-start(f32[4,2560,128,4]{2,1,3,0:T(8,128)S(1)} %get-tuple-element.31) | copy-start | bytes 62914564
  251.8 7.1 %copy-start.8 = (bf16[128,2048]{0,1:T(8,128)(2,1)S(1)}, bf16[128,2048]{0,1:T(8,128)(2,1)}, u32[]{:S(2)}) copy-start(bf16[128,2048]{0,1:T(8,128)(2,1)} %copy.217) | copy-start | bytes 1572868
  258.9 11.9 %copy-start.6 = (bf16[20,128,4,128]{3,1,0,2:T(8,128)(2,1)S(1)}, bf16[20,128,4,128]{3,1,0,2:T(8,128)(2,1)}, u32[]{:S(2)}) copy-start(bf16[20,128,4,128]{3,1,0,2:T(8,128)(2,1)} %copy.175) | copy-start | bytes 7864324
  317.1 9.8 %copy-start.13 = (s32[20]{0:T(128)S(1)}, s32[20]{0:T(128)}, u32[]{:S(2)}) copy-start(s32[20]{0:T(128)} %copy-done.12) | copy-start | bytes 244
  340.7 17.9 %copy-start.11 = (s32[20]{0:T(128)S(1)}, s32[20]{0:T(128)}, u32[]{:S(2)}) copy-start(s32[20]{0:T(128)} %copy-done.10) | copy-start | bytes 244
Sparse Core Ops, SparseCore 0:
  9.5 35.8 all-gather.8
  48.2 50.5 all-gather.6
  100.9 49.0 all-gather.4
  398.8 177.1 reduce-scatter.1
where the time goes:
time: 596 us; the launch traced here: 586 us
  waiting for transfers between devices  239 us (40%)
  matrix products  135 us (23%)
  local copies, waits for them, and re-layouts  98 us (16%)
  other arithmetic  76.3 us (13%)
  blocking collectives  23.1 us (4%)
  between operations  14.5 us (2%)
    reduce_scatter x1, waiting for transfers between devices, on_device(): home = lax.psum_scatter(combined, 'ctx', scatter_dimension=0, tiled=True)  157 us
    all_gather x1, waiting for transfers between devices, on_device(): lax.all_gather(value, 'ctx', axis=0, tiled=True)  40.3 us
    all_gather x1, waiting for transfers between devices, on_device(): lax.all_gather(key, 'ctx', axis=0, tiled=True)  38.4 us
    dot_general x2, matrix products, on_device(): jnp.einsum('gnij,jgd->ignd', probs, v_near.astype(jnp.float32), precision...  33.4 us
    dot_general x2, matrix products, backward_pair(): jnp.einsum('ignd,jgd->gnij', do_block, v_block, preferred_element_type=jn...  30.2 us
    scatter-add x2, other arithmetic, on_device(): grad_k_all.at[listed].add(part_k.reshape(slots, BLK, kv_here, width))  27.4 us
    scatter-add x2, other arithmetic, on_device(): grad_v_all.at[listed].add(part_v.reshape(slots, BLK, kv_here, width))  27.2 us
    dot_general x2, matrix products, backward_pair(): jnp.einsum('gnij,ignd->jgd', rounded, do_block, preferred_element_type=jn...  23.7 us
  transfers between devices with their start and end apart: 4, of which 4 were waited for; matrix products, arithmetic and copies ran while one was open for 10% of the time, Pallas kernels for 0%

commit v1 on v0

--- a/solution.py
+++ b/solution.py
@@ -1,3 +1,4 @@
+import functools
 import math
 import jax
 import jax.numpy as jnp
@@ -5,6 +6,21 @@
 from jax.sharding import PartitionSpec as P
 
 BLK = 128
+
+
+def list_layers_all_up(field, k_dim):
+    b_now, piece_now = (lax.axis_size("ctx"), lax.axis_index("ctx"))
+    step_out, top = (field, 1)
+    while top < b_now:
+        z_new = lax.ppermute(step_out, "ctx", [(q, q ^ top) for q in range(b_now)])
+        current_block = jnp.concatenate([step_out, z_new], axis=k_dim)
+        extra = jnp.concatenate([z_new, step_out], axis=k_dim)
+        step_out = jnp.where(piece_now & top == 0, current_block, extra)
+        top = 2 * top
+    return step_out
+
+
+blocks_pass = functools.partial(list_layers_all_up, k_dim=0)
 
 
 def score_pair(q_block, scope_q, k_block, scope_k, scale):
@@ -48,7 +64,7 @@
     do_blocks = d_out.reshape(blocks, BLK, kv_here, group, width)
     own_scope = scope_ids.reshape(blocks, BLK).astype(jnp.float32)
     all_keys, all_values, all_scope = (
-        lax.all_gather(key, "ctx", axis=0, tiled=True),
+        blocks_pass(key),
         lax.all_gather(value, "ctx", axis=0, tiled=True),
         lax.all_gather(scope_ids.astype(jnp.bfloat16), "ctx", axis=0, tiled=True),
     )

time: 596 us -> 682 us (1.14)
  other arithmetic: 76.3 us -> 119 us
  waiting for transfers between devices: 239 us -> 277 us
    ppermute x0 -> x4, waiting for transfers between devices: none -> 120 us  [list_layers_all_up(): z_new = lax.ppermute(step_out, 'ctx', [(q, q ^ top) for q in range(b_now)])]
    select_n x0 -> x4, other arithmetic: none -> 42.9 us  [list_layers_all_up(): step_out = jnp.where(piece_now & top == 0, current_block, extra)]
    all_gather x1, waiting for transfers between devices: 40.3 us -> 0.01 us  [on_device(): lax.all_gather(value, 'ctx', axis=0, tiled=True)]
    all_gather x1 -> x0, waiting for transfers between devices: 38.4 us -> none  [on_device(): lax.all_gather(key, 'ctx', axis=0, tiled=True)]
  transfers between devices with their start and end apart: 4 -> 7, of which waited for: 4 -> 4; matrix products, arithmetic and copies ran while one was open for 10% -> 31% of each run, Pallas kernels for 0% -> 0%
where the time goes in v1:
time: 682 us; the launch traced here: 673 us
  waiting for transfers between devices  277 us (41%)
  matrix products  137 us (20%)
  other arithmetic  119 us (17%)
  local copies, waits for them, and re-layouts  103 us (15%)
  blocking collectives  22.6 us (3%)
  between operations  14.3 us (2%)
    reduce_scatter x1, waiting for transfers between devices, on_device(): home = lax.psum_scatter(combined, 'ctx', scatter_dimension=0, tiled=True)  156 us
    ppermute x4, waiting for transfers between devices, list_layers_all_up(): z_new = lax.ppermute(step_out, 'ctx', [(q, q ^ top) for q in range(b_now)])  120 us
    select_n x4, other arithmetic, list_layers_all_up(): step_out = jnp.where(piece_now & top == 0, current_block, extra)  42.9 us
    dot_general x2, matrix products, on_device(): jnp.einsum('gnij,jgd->ignd', probs, v_near.astype(jnp.float32), precision...  33.9 us
    dot_general x2, matrix products, backward_pair(): jnp.einsum('ignd,jgd->gnij', do_block, v_block, preferred_element_type=jn...  30.4 us
    scatter-add x2, other arithmetic, on_device(): grad_k_all.at[listed].add(part_k.reshape(slots, BLK, kv_here, width))  27.3 us
    scatter-add x2, other arithmetic, on_device(): grad_v_all.at[listed].add(part_v.reshape(slots, BLK, kv_here, width))  27.3 us
    dot_general x2, matrix products, backward_pair(): jnp.einsum('gnij,ignd->jgd', rounded, do_block, preferred_element_type=jn...  23.4 us
  transfers between devices with their start and end apart: 7, of which 4 were waited for; matrix products, arithmetic and copies ran while one was open for 31% of the time, Pallas kernels for 0%

profile of v1, /device:TPU:0, one launch (start us, length us, event | category | flops | bytes accessed | tf_op | source)
XLA Modules:
  0.0 673.5 jit_solution(8169810487055574525)
XLA Ops:
  11.8 22.6 %all-gather = bf16[16,1,256]{2,1,0:T(2,128)(2,1)S(1)} all-gather(bf16[1,1,256]{2,1,0:T(2,128)(2,1)S(1)} %reshape.255), channel_id=1, replica_groups=mesh['ctx'=16,'head'=2] {'ctx'}, dimensions={0}, use_global_device_ids=true | all-gather | bytes 8704 | tf_op jit(solution)/shard_map/all_gather | solution.py:69
  39.2 12.4 %collective-permute-done.1 = bf16[512,4,128]{2,1,0:T(4,128)(2,1)S(1)} collective-permute-done((bf16[512,4,128]{2,1,0:T(4,128)(2,1)S(1)}, bf16[512,4,128]{2,1,0:T(4,128)(2,1)S(1)}, u32[]{:S(2)}, u32[]{:S(2)}) %collective-permute-start.1) | collective-permute-done | bytes 524320 | tf_op jit(solution)/shard_map/ppermute | solution.py:15
  54.6 39.1 %collective-permute-done.2 = bf16[1024,4,128]{2,1,0:T(4,128)(2,1)S(1)} collective-permute-done((bf16[1024,4,128]{2,1,0:T(4,128)(2,1)S(1)}, bf16[1024,4,128]{2,1,0:T(4,128)(2,1)S(1)}, u32[]{:S(2)}, u32[]{:S(2)}) %collective-permute-start.2) | collective-permute-done | bytes 1048608 | tf_op jit(solution)/shard_map/ppermute | solution.py:15
  93.7 12.9 %maximum_select_fusion.1 = bf16[2048,4,128]{2,1,0:T(4,128)(2,1)S(1)} fusion(bf16[1024,4,128]{2,1,0:T(4,128)(2,1)S(1)} %collective-permute-done.2, bf16[1024,4,128]{2,1,0:T(4,128)(2,1)S(1)} %maximum_select_fusion.2, pred[]{:T(512)S(6)} %eq.35), kind=kLoop, calls=%fused_computation.57 | loop fusion | flops 3145728 | bytes 4194305 | tf_op jit(solution)/shard_map/jit(_where)/select_n | solution.py:18
  108.7 11.9 %convolution_convert_fusion = bf16[256,2048]{1,0:T(8,128)(2,1)} fusion(bf16[256,4096]{1,0:T(8,128)(2,1)} %all-gather.6.cloned.1.call-done, bf16[2048,4096]{1,0:T(8,128)(2,1)} %param.11), kind=kOutput, calls=%fused_computation.56 | convolution fusion | flops 4295491584 | bytes 19922944 | tf_op jit(solution)/shard_map/dot_general | solution.py:57
  120.7 2.1 fusion.74
  122.7 2.1 copy.216
  125.8 68.4 %collective-permute-done.3 = bf16[2048,4,128]{2,1,0:T(4,128)(2,1)} collective-permute-done((bf16[2048,4,128]{2,1,0:T(4,128)(2,1)S(1)}, bf16[2048,4,128]{2,1,0:T(4,128)(2,1)}, u32[]{:S(2)}, u32[]{:S(2)}) %collective-permute-start.3) | collective-permute-done | bytes 2097184 | tf_op jit(solution)/shard_map/ppermute | solution.py:15
  194.2 27.1 %maximum_select_fusion = bf16[4096,4,128]{2,1,0:T(4,128)(2,1)} fusion(bf16[2048,4,128]{2,1,0:T(4,128)(2,1)} %collective-permute-done.3, bf16[2048,4,128]{2,1,0:T(4,128)(2,1)S(1)} %maximum_select_fusion.1, pred[]{:T(512)S(6)} %eq.34), kind=kLoop, calls=%fused_computation.55 | loop fusion | flops 6291456 | bytes 8388609 | tf_op jit(solution)/shard_map/jit(_where)/select_n | solution.py:18
  221.3 7.6 %gather_fusion.3 = bf16[20,128,4,128]{3,2,1,0:T(4,128)(2,1)} fusion(bf16[32,128,4,128]{3,2,1,0:T(4,128)(2,1)} %bitcast.207, s32[1024]{0:T(1024)S(1)} %get-tuple-element.34), kind=kCustom, calls=%fused_computation.3 | custom fusion | bytes 5242960 | tf_op jit(solution)/shard_map/gather | solution.py:81
  229.0 7.4 %gather_fusion = bf16[20,128,4,128]{3,2,1,0:T(4,128)(2,1)} fusion(bf16[32,128,4,128]{3,2,1,0:T(4,128)(2,1)} %bitcast.208, s32[1024]{0:T(1024)S(1)} %get-tuple-element.35), kind=kCustom, calls=%fused_computation | custom fusion | bytes 5242960 | tf_op jit(solution)/shard_map/gather | solution.py:81
  236.4 2.5 copy.162
  238.8 3.9 copy.172
  242.8 4.5 fusion.3
  247.3 4.3 fusion.6
  251.6 2.8 copy-done
  254.4 11.7 %fusion.41 = f32[2560,4,128]{0,2,1:T(8,128)} fusion(bf16[128,4,4,128]{0,3,2,1:T(8,128)(2,1)S(1)} %bitcast.226, f32[4,2560,128,4]{2,1,3,0:T(8,128)} %copy-done, f32[4,4,128]{2,1,0:T(4,128)S(1)} %bitcast.233, pred[128,2560]{0,1:T(8,128)(4,1)S(1)} %compare_or_fusion), kind=kOutput, calls=%fused_computation.54 | convolution fusion | flops 1363148800 | bytes 27074560 | tf_op jit(solution)/shard_map/gnij,ignd->jgd/dot_general | solution.py:41
  266.1 6.2 copy.190
  272.3 5.5 copy.191
  277.8 3.0 fusion.12
  280.9 4.3 fusion.15
  285.2 2.8 copy-done.1
  287.9 11.7 %fusion.38 = f32[2560,4,128]{0,2,1:T(8,128)} fusion(bf16[128,4,4,128]{0,3,2,1:T(8,128)(2,1)S(1)} %bitcast.223, f32[4,2560,128,4]{2,1,3,0:T(8,128)} %copy-done.1, f32[4,4,128]{2,1,0:T(4,128)S(1)} %bitcast.236, pred[128,2560]{0,1:T(8,128)(4,1)S(1)} %compare_or_fusion.1), kind=kOutput, calls=%fused_computation.53 | convolution fusion | flops 1363148800 | bytes 27074560 | tf_op jit(solution)/shard_map/gnij,ignd->jgd/dot_general | solution.py:41
  299.6 6.0 copy.186
  305.6 5.4 copy.187
  311.0 4.3 broadcast.72.clone
  315.3 13.6 %scatter_fusion.2 = f32[32,128,4,128]{3,1,2,0:T(8,128)} fusion(f32[32,128,4,128]{3,1,2,0:T(8,128)} %broadcast.72.clone, s32[20]{0:T(128)S(1)} %get-tuple-element.26, f32[20,128,4,128]{3,1,2,0:T(8,128)} %copy.187), kind=kCustom, calls=%fused_computation.8 | custom fusion | flops 1310720 | bytes 15728720 | tf_op jit(solution)/shard_map/scatter-add | solution.py:108
  329.0 13.6 %scatter_fusion.3 = f32[32,128,4,128]{3,1,2,0:T(8,128)} fusion(f32[32,128,4,128]{3,1,2,0:T(8,128)} %scatter_fusion.2, s32[20]{0:T(128)S(1)} %get-tuple-element.27, f32[20,128,4,128]{3,1,2,0:T(8,128)} %copy.191), kind=kCustom, calls=%fused_computation.9 | custom fusion | flops 1310720 | bytes 15728720 | tf_op jit(solution)/shard_map/scatter-add | solution.py:108
  342.6 4.7 copy.165
  347.3 4.8 gather_fusion.2
  352.0 4.7 gather_fusion.5
  356.8 2.1 copy.175
  360.9 17.1 %fusion.58 = f32[128,4,4]{0,2,1:T(4,128)S(1)} fusion(bf16[2560,4,128,1]{2,0,3,1:T(8,128)(2,1)S(1)} %bitcast.221, f32[4,2560,128,4]{2,1,3,0:T(8,128)} %copy-done, f32[4,4,128]{2,1,0:T(4,128)S(1)} %bitcast.234, pred[128,2560]{0,1:T(8,128)(4,1)S(1)} %compare_or_fusion, bf16[128,4,4,128]{0,3,2,1:T(8,128)(2,1)S(1)} %bitcast.227), kind=kOutput, calls=%fused_computation.68 | convolution fusion | flops 8069576704 | bytes 24461312 | tf_op jit(solution)/shard_map/gnij,jgd->ignd/dot_general | solution.py:90
  378.0 15.2 %fusion.2 = bf16[4,4,128,2560]{2,3,1,0:T(8,128)(2,1)} fusion(f32[4,2560,128,4]{2,1,3,0:T(8,128)} %copy-done, f32[4,4,128]{2,1,0:T(4,128)S(1)} %bitcast.239, f32[4,4,128]{2,1,0:T(4,128)S(1)} %bitcast.235, pred[128,2560]{0,1:T(8,128)(4,1)S(1)} %compare_or_fusion, bf16[2560,4,128,1]{2,0,3,1:T(8,128)(2,1)S(1)} %bitcast.222, ...), kind=kOutput, calls=%fused_computation.13 | convolution fusion | flops 1378877440 | bytes 34947072 | tf_op jit(solution)/shard_map/ignd,jgd->gnij/dot_general | solution.py:42
  393.2 5.6 fusion.80
  398.8 3.0 copy.183
  401.8 16.8 %fusion.61 = f32[128,4,4]{0,2,1:T(4,128)S(1)} fusion(bf16[2560,4,128,1]{2,0,3,1:T(8,128)(2,1)S(1)} %bitcast.219, f32[4,2560,128,4]{2,1,3,0:T(8,128)} %copy-done.1, f32[4,4,128]{2,1,0:T(4,128)S(1)} %bitcast.237, pred[128,2560]{0,1:T(8,128)(4,1)S(1)} %compare_or_fusion.1, bf16[128,4,4,128]{0,3,2,1:T(8,128)(2,1)S(1)} %bitcast.224), kind=kOutput, calls=%fused_computation.69 | convolution fusion | flops 8069576704 | bytes 24461312 | tf_op jit(solution)/shard_map/gnij,jgd->ignd/dot_general | solution.py:90
  418.6 15.3 %fusion.11 = bf16[4,4,128,2560]{2,3,1,0:T(8,128)(2,1)} fusion(f32[4,2560,128,4]{2,1,3,0:T(8,128)} %copy-done.1, f32[4,4,128]{2,1,0:T(4,128)S(1)} %bitcast.240, f32[4,4,128]{2,1,0:T(4,128)S(1)} %bitcast.238, pred[128,2560]{0,1:T(8,128)(4,1)S(1)} %compare_or_fusion.1, bf16[2560,4,128,1]{2,0,3,1:T(8,128)(2,1)S(1)} %bitcast.220, ...), kind=kOutput, calls=%fused_computation.26 | convolution fusion | flops 1378877440 | bytes 34947072 | tf_op jit(solution)/shard_map/ignd,jgd->gnij/dot_general | solution.py:42
  433.9 5.6 fusion.79
  439.5 2.9 copy.182
  442.4 4.3 broadcast.72.clone.1
  446.7 13.8 %scatter_fusion = f32[32,128,4,128]{3,1,2,0:T(8,128)} fusion(f32[32,128,4,128]{3,1,2,0:T(8,128)} %broadcast.72.clone.1, s32[20]{0:T(128)S(1)} %get-tuple-element.26, f32[20,128,4,128]{3,1,2,0:T(8,128)} %copy.182), kind=kCustom, calls=%fused_computation.6 | custom fusion | flops 1310720 | bytes 15728720 | tf_op jit(solution)/shard_map/scatter-add | solution.py:107
  460.5 13.6 %scatter_fusion.1 = f32[32,128,4,128]{3,1,2,0:T(8,128)} fusion(f32[32,128,4,128]{3,1,2,0:T(8,128)} %scatter_fusion, s32[20]{0:T(128)S(1)} %get-tuple-element.27, f32[20,128,4,128]{3,1,2,0:T(8,128)} %copy.183), kind=kCustom, calls=%fused_computation.7 | custom fusion | flops 1310720 | bytes 15728720 | tf_op jit(solution)/shard_map/scatter-add | solution.py:107
  474.1 6.6 pad_maximum_fusion
  480.7 6.2 copy.192
  486.9 9.1 %fusion.57 = bf16[1,128,4,4,128]{4,1,3,2,0:T(8,128)(2,1)S(1)} fusion(bf16[2560,4,128,1]{2,0,3,1:T(8,128)(2,1)} %bitcast.206, bf16[4,4,128,2560]{2,3,1,0:T(8,128)(2,1)} %fusion.2), kind=kOutput, calls=%fused_computation.67 | convolution fusion | flops 1342439424 | bytes 13631488 | tf_op jit(solution)/shard_map/gnij,jgd->ignd/dot_general | solution.py:44
  496.0 9.4 %fusion.56 = bf16[1,128,4,4,128]{4,1,3,2,0:T(8,128)(2,1)S(1)} fusion(bf16[2560,4,128,1]{2,0,3,1:T(8,128)(2,1)S(1)} %bitcast.204, bf16[4,4,128,2560]{2,3,1,0:T(8,128)(2,1)} %fusion.11), kind=kOutput, calls=%fused_computation.66 | convolution fusion | flops 1342439424 | bytes 13631488 | tf_op jit(solution)/shard_map/gnij,jgd->ignd/dot_general | solution.py:44
  507.3 156.2 %reduce-scatter.2.cloned.1.call-done = f32[256,4,256]{2,0,1:T(8,128)} async-done(((f32[4096,4,256]{2,0,1:T(8,128)}), f32[256,4,256]{2,0,1:T(8,128)}) %reduce-scatter.2.cloned.1.call-update) | async-done | bytes 1048592 | tf_op jit(solution)/shard_map/reduce_scatter | solution.py:112
  (65 shorter events, 22.6 us)
Async XLA Ops:
  7.2 101.6 %all-gather.6.cloned.1.call-start = ((), (), s32[]{:S(2)}) async-start(), calls=%async_computation.2 | async-start | bytes 3145728 | tf_op jit(solution)/shard_map/all_gather | solution.py:58
  7.9 334.7 %all-gather.4.cloned.1.call-start = ((), (), s32[]{:S(2)}) async-start(), calls=%async_computation.1 | async-start | bytes 4456448 | tf_op jit(solution)/shard_map/all_gather | solution.py:68
  7.9 27.7 %collective-permute-start = (bf16[256,4,128]{2,1,0:T(4,128)(2,1)}, bf16[256,4,128]{2,1,0:T(4,128)(2,1)S(1)}, u32[]{:S(2)}, u32[]{:S(2)}) collective-permute-start(bf16[256,4,128]{2,1,0:T(4,128)(2,1)} %param.8), channel_id=1, source_target_pairs={{0,2},{2,0},{4,6},{6,4},{8,10},{10,8},{12,14},{14,12},{16,18},{18,... | collective-permute-start | bytes 786440 | tf_op jit(solution)/shard_map/ppermute | solution.py:15
  10.2 653.3 %reduce-scatter.2.cloned.1.call-start = ((), (), s32[]{:S(2)}) async-start(), calls=%async_computation.3 | async-start | bytes 17825792 | tf_op jit(solution)/shard_map/reduce_scatter | solution.py:112
  35.6 71.0 %copy-start.6 = (bf16[256,16,128]{2,1,0:T(8,128)(2,1)S(1)}, bf16[256,16,128]{2,1,0:T(8,128)(2,1)}, u32[]{:S(2)}) copy-start(bf16[256,16,128]{2,1,0:T(8,128)(2,1)} %param.7) | copy-start | bytes 3145732
  37.4 14.2 %collective-permute-start.1 = (bf16[512,4,128]{2,1,0:T(4,128)(2,1)S(1)}, bf16[512,4,128]{2,1,0:T(4,128)(2,1)S(1)}, u32[]{:S(2)}, u32[]{:S(2)}) collective-permute-start(bf16[512,4,128]{2,1,0:T(4,128)(2,1)S(1)} %maximum_select_fusion.3), channel_id=1, source_target_pairs={{0,4},{2,6},{4,0},{6,2},{8,12},{10,14},{12,8},{14,10},{16,20},{18,... | collective-permute-start | bytes 1572872 | tf_op jit(solution)/shard_map/ppermute | solution.py:15
  52.7 40.9 %collective-permute-start.2 = (bf16[1024,4,128]{2,1,0:T(4,128)(2,1)S(1)}, bf16[1024,4,128]{2,1,0:T(4,128)(2,1)S(1)}, u32[]{:S(2)}, u32[]{:S(2)}) collective-permute-start(bf16[1024,4,128]{2,1,0:T(4,128)(2,1)S(1)} %maximum_select_fusion.2), channel_id=1, source_target_pairs={{0,8},{2,10},{4,12},{6,14},{8,0},{10,2},{12,4},{14,6},{16,24},{18,... | collective-permute-start | bytes 3145736 | tf_op jit(solution)/shard_map/ppermute | solution.py:15
  106.6 87.7 %collective-permute-start.3 = (bf16[2048,4,128]{2,1,0:T(4,128)(2,1)S(1)}, bf16[2048,4,128]{2,1,0:T(4,128)(2,1)}, u32[]{:S(2)}, u32[]{:S(2)}) collective-permute-start(bf16[2048,4,128]{2,1,0:T(4,128)(2,1)S(1)} %maximum_select_fusion.1), channel_id=1, source_target_pairs={{0,16},{2,18},{4,20},{6,22},{8,24},{10,26},{12,28},{14,30},{16,0},... | collective-permute-start | bytes 6291464 | tf_op jit(solution)/shard_map/ppermute | solution.py:15
  236.4 6.4 copy-start.4
  247.3 7.1 %copy-start = (f32[4,2560,128,4]{2,1,3,0:T(8,128)}, f32[4,2560,128,4]{2,1,3,0:T(8,128)S(1)}, u32[]{:S(2)}) copy-start(f32[4,2560,128,4]{2,1,3,0:T(8,128)S(1)} %get-tuple-element.31) | copy-start | bytes 62914564
  247.3 7.1 %copy-start.9 = (bf16[128,2048]{0,1:T(8,128)(2,1)S(1)}, bf16[128,2048]{0,1:T(8,128)(2,1)}, u32[]{:S(2)}) copy-start(bf16[128,2048]{0,1:T(8,128)(2,1)} %copy.217) | copy-start | bytes 1572868
  272.3 5.6 copy-start.2
  280.8 7.1 %copy-start.1 = (f32[4,2560,128,4]{2,1,3,0:T(8,128)}, f32[4,2560,128,4]{2,1,3,0:T(8,128)S(1)}, u32[]{:S(2)}) copy-start(f32[4,2560,128,4]{2,1,3,0:T(8,128)S(1)} %get-tuple-element.33) | copy-start | bytes 62914564
  280.8 7.1 %copy-start.7 = (bf16[128,2048]{0,1:T(8,128)(2,1)S(1)}, bf16[128,2048]{0,1:T(8,128)(2,1)}, u32[]{:S(2)}) copy-start(bf16[128,2048]{0,1:T(8,128)(2,1)} %copy.216) | copy-start | bytes 1572868
  356.8 4.2 copy-start.10
  378.0 15.2 %copy-start.5 = (bf16[128,16,128]{2,0,1:T(8,128)(2,1)S(1)}, bf16[128,16,128]{2,0,1:T(8,128)(2,1)}, u32[]{:S(2)}) copy-start(bf16[128,16,128]{2,0,1:T(8,128)(2,1)} %copy.173) | copy-start | bytes 1572868
  398.8 3.0 copy-start.8
  418.6 15.3 %copy-start.3 = (bf16[128,16,128]{2,0,1:T(8,128)(2,1)S(1)}, bf16[128,16,128]{2,0,1:T(8,128)(2,1)}, u32[]{:S(2)}) copy-start(bf16[128,16,128]{2,0,1:T(8,128)(2,1)} %copy.163) | copy-start | bytes 1572868
Sparse Core Ops, SparseCore 0:
  9.5 35.8 all-gather.5
  48.2 60.8 all-gather.3
  487.0 176.4 reduce-scatter.1
